TPU v7x, 32 devices: a whole 2x2x4 slice. The times are simulated.
32 devices in a mesh: uly: 8 (over z, y), blk: 4 (over x, core).
Axes of the slice: x: 2, y: 2, z: 4, core: 2. Of those that a mesh axis runs over, the one named last changes fastest.
Arguments:
- qkv: bfloat16 [8192, 6144], P(('blk', 'uly')), may hold values from -16 to 16
- tile_list: int32 [32, 8], P('blk'), may hold values from 0 to 31, as said below
Outputs:
- attended: bfloat16 [8192, 2048], P(('blk', 'uly'))
Inputs may be any that keep to these rules, and one draw needn't show every extreme that they name: Let the frame of tile t be t // 8, its row t % 8 // 4 and its column t % 4. Each row of tile_list names 8 distinct tiles: its own tile and others whose frame, row and column each differ from its own by at most one.
All inputs are finite; a program needn't handle non-finite values.
Results may differ from a plain program's by a relative error of at most 0.0047.
Values may be sent and summed in bfloat16 or wider, within the bound.
A program may use at most 128 MiB of HBM per device.

v0:
```python
import math

import jax
import jax.numpy as jnp
from jax import lax
from jax.sharding import PartitionSpec as P

HEAD_DIM = 64


def with_halo(cells, sides, width):
    for axis, dim in sides:
        count = lax.axis_size(axis)
        ends = count - 1
        head = lax.slice_in_dim(cells, 0, width, axis=dim)
        tail = lax.slice_in_dim(cells, cells.shape[dim] - width, cells.shape[dim], axis=dim)
        cells = jnp.concatenate(
            [
                lax.ppermute(tail, axis, [(i, (i + 1) % count) for i in range(ends)]),
                cells,
                lax.ppermute(head, axis, [((i + 1) % count, i) for i in range(ends)]),
            ],
            axis=dim,
        )
    return cells


def attend_group(queries, window, listed, score_scale):
    picked = window[listed]
    head_width = queries.shape[-1]
    key_part = picked[..., :head_width]
    val_part = picked[..., head_width:]
    scores = (
        jnp.einsum("gqhd,gjkhd->ghqjk", queries, key_part, preferred_element_type=jnp.float32)
        * score_scale
    )
    row_max = jnp.max(scores, axis=(3, 4), keepdims=True)
    exponent = jnp.exp(scores - row_max)
    row_sum = jnp.sum(exponent, axis=(3, 4))
    weights = exponent.astype(jnp.bfloat16)
    summed = jnp.einsum("ghqjk,gjkhd->gqhd", weights, val_part, preferred_element_type=jnp.float32)
    return (summed / jnp.transpose(row_sum, (0, 2, 1))[..., None]).astype(jnp.bfloat16)


def on_device(qkv, tile_list):
    score_scale = HEAD_DIM ** (-0.5)
    token_count = qkv.shape[0]
    all_heads = qkv.shape[1] // (3 * HEAD_DIM)
    head_here = all_heads // lax.axis_size("uly")
    row_count = token_count * lax.axis_size("uly")
    by_head = lax.all_to_all(qkv, "uly", split_axis=1, concat_axis=0, tiled=True)
    by_head = by_head.reshape(row_count, head_here, 3 * HEAD_DIM)
    queries = by_head[:, :, :HEAD_DIM]
    keyvals = by_head[:, :, HEAD_DIM:]
    window = with_halo(keyvals, (("blk", 0),), row_count)
    frame_tiles = tile_list.shape[0]
    tile_len = row_count // frame_tiles
    first_tile = (lax.axis_index("blk") - 1) * frame_tiles
    window = window.reshape(window.shape[0] // tile_len, tile_len, head_here, 2 * HEAD_DIM)
    local_list = tile_list - first_tile
    group_size = math.gcd(frame_tiles, max(1, 512 // tile_len))
    query_groups = queries.reshape(
        frame_tiles // group_size, group_size, tile_len, head_here, HEAD_DIM
    )
    list_groups = local_list.reshape(frame_tiles // group_size, group_size, local_list.shape[1])

    def run_group(inputs):
        return attend_group(inputs[0], window, inputs[1], score_scale)

    result = lax.map(run_group, (query_groups, list_groups))
    result = result.reshape(row_count, head_here * HEAD_DIM)
    return lax.all_to_all(result, "uly", split_axis=0, concat_axis=1, tiled=True)


def solution(mesh):
    in_specs = (P(("blk", "uly"), None), P("blk", None))
    out_specs = P(("blk", "uly"), None)
    return jax.shard_map(
        on_device, mesh=mesh, in_specs=in_specs, out_specs=out_specs, check_vma=False
    )
```

profile of v0, /device:TPU:1, one launch (start us, length us, event | category | flops | bytes accessed | tf_op | source)
XLA Modules:
  0.0 295.7 jit_solution(18206728931331256249)
XLA Ops:
  3.2 76.0 %all_to_all.35 = bf16[256,8,768]{0,2,1:T(8,128)(2,1)S(1)} all-to-all(bf16[256,8,768]{0,2,1:T(8,128)(2,1)S(1)} %bitcast.64), channel_id=1, replica_groups=mesh['uly'=8,'blk'=4] {'uly'}, dimensions={1} | all-to-all | bytes 6291456 | tf_op jit(solution)/shard_map/all_to_all | solution.py:51
  98.2 18.2 %collective-permute-done = bf16[2048,4,128]{0,2,1:T(8,128)(2,1)} collective-permute-done((bf16[2048,4,128]{0,2,1:T(8,128)(2,1)}, bf16[2048,4,128]{0,2,1:T(8,128)(2,1)}, u32[]{:S(2)}, u32[]{:S(2)}) %collective-permute-start) | collective-permute-done | bytes 2097184 | tf_op jit(solution)/shard_map/ppermute | solution.py:19
  129.3 9.1 %copy.33 = bf16[24,256,4,128]{3,1,2,0:T(8,128)(2,1)} copy(bf16[24,256,4,128]{1,0,3,2:T(8,128)(2,1)} %bitcast.62) | data formatting | bytes 12582912 | tf_op jit(solution)/shard_map/while | solution.py:70
  138.4 137.0 %while.10 = (s32[]{:T(128)}, bf16[4,2,256,4,64]{2,4,3,1,0:T(8,128)(2,1)S(1)}, s32[4,2,8]{2,1,0:T(2,128)S(1)}, bf16[24,256,4,128]{3,1,2,0:T(8,128)(2,1)}, bf16[4,2,256,4,64]{2,1,0,4,3:T(2,128)(2,1)S(1)}, /*index=5*/s32[]{:T(128)}) while((s32[]{:T(128)}, bf16[4,2,256,4,64]{2,4,3,1,0:T(8,128)(2,1)S(1)}, s32[4,2,8]{2,1,0:T(2,128)S(1)}, ...), condition=%wide.region_3.4_spmd, body=%wide.region_0.3_spmd.sunk | while | flops 1107555328 | bytes 74494416 | solution.py:70
  138.5 5.8 %gather_fusion = bf16[16,256,4,128]{3,1,2,0:T(8,128)(2,1)} fusion(bf16[24,256,4,128]{3,1,2,0:T(8,128)(2,1)} %get-tuple-element.121, s32[1024]{0:T(1024)S(1)} %pad_clamp_fusion.2), kind=kCustom, calls=%fused_computation.clone.1 | custom fusion | bytes 8388672 | tf_op jit(solution)/shard_map/while/body/eval_jaxpr/gather | solution.py:29
  144.3 5.0 %fusion.43 = (bf16[2,8,256,4,64]{4,2,3,1,0:T(8,128)(2,1)S(1)}, bf16[2,8,256,4,64]{4,2,3,1,0:T(8,128)(2,1)S(1)}) fusion(bf16[2,8,256,4,128]{4,2,3,1,0:T(8,128)(2,1)} %bitcast.60), kind=kLoop, calls=%fused_computation.23.clone.1 | loop fusion | bytes 8388608 | tf_op jit(solution)/shard_map/while/body/eval_jaxpr/slice | solution.py:32
  149.5 7.0 %multiply_reduce_fusion.2 = (f32[2,4,256]{2,1,0:T(4,128)S(1)}, f32[2,4,256,8,256]{2,4,3,1,0:T(8,128)}) fusion(bf16[2,8,256,4,64]{4,2,3,1,0:T(8,128)(2,1)S(1)} %get-tuple-element.102, bf16[1,2,256,4,64]{2,1,0,4,3:T(2,128)(2,1)S(1)} %constant_dynamic-slice_fusion.2), kind=kOutput, calls=%fused_computation.2.clone.1 | convolution fusion | flops 545257472 | bytes 19144704 | tf_op jit(solution)/shard_map/while/body/eval_jaxpr/gqhd,gjkhd->ghqjk/dot_general | solution.py:34
  156.5 8.5 %fusion.44 = f32[2,4,256]{2,1,0:T(4,128)S(1)} fusion(f32[2,4,256,8,256]{2,4,3,1,0:T(8,128)} %get-tuple-element.103, f32[2,4,256]{2,1,0:T(4,128)S(1)} %get-tuple-element.104), kind=kLoop, calls=%fused_computation.3.clone.1 | loop fusion | flops 12580864 | bytes 16793600 | tf_op jit(solution)/shard_map/while/body/eval_jaxpr/reduce_sum | solution.py:39
  165.0 7.5 %fusion.45 = bf16[4,2,256,4,64]{2,4,3,1,0:T(8,128)(2,1)S(1)} fusion(bf16[4,2,256,4,64]{2,4,3,1,0:T(8,128)(2,1)S(1)} %get-tuple-element.113, s32[]{:T(128)} %get-tuple-element.112, f32[2,4,256,8,256]{2,4,3,1,0:T(8,128)} %get-tuple-element.103, f32[2,4,256]{2,1,0:T(4,128)S(1)} %get-tuple-element.104, ...), kind=kOutput, calls=%fused_computation.15.clone.1 | convolution fusion | flops 549715968 | bytes 21250052 | tf_op jit(solution)/shard_map/while/body/eval_jaxpr/ghqjk,gjkhd->gqhd/dot_general | solution.py:41
  172.7 5.8 %gather_fusion = bf16[16,256,4,128]{3,1,2,0:T(8,128)(2,1)} fusion(bf16[24,256,4,128]{3,1,2,0:T(8,128)(2,1)} %get-tuple-element.121, s32[1024]{0:T(1024)S(1)} %pad_clamp_fusion.2), kind=kCustom, calls=%fused_computation.clone.1 | custom fusion | bytes 8388672 | tf_op jit(solution)/shard_map/while/body/eval_jaxpr/gather | solution.py:29
  178.5 5.0 %fusion.43 = (bf16[2,8,256,4,64]{4,2,3,1,0:T(8,128)(2,1)S(1)}, bf16[2,8,256,4,64]{4,2,3,1,0:T(8,128)(2,1)S(1)}) fusion(bf16[2,8,256,4,128]{4,2,3,1,0:T(8,128)(2,1)} %bitcast.60), kind=kLoop, calls=%fused_computation.23.clone.1 | loop fusion | bytes 8388608 | tf_op jit(solution)/shard_map/while/body/eval_jaxpr/slice | solution.py:32
  183.8 7.0 %multiply_reduce_fusion.2 = (f32[2,4,256]{2,1,0:T(4,128)S(1)}, f32[2,4,256,8,256]{2,4,3,1,0:T(8,128)}) fusion(bf16[2,8,256,4,64]{4,2,3,1,0:T(8,128)(2,1)S(1)} %get-tuple-element.102, bf16[1,2,256,4,64]{2,1,0,4,3:T(2,128)(2,1)S(1)} %constant_dynamic-slice_fusion.2), kind=kOutput, calls=%fused_computation.2.clone.1 | convolution fusion | flops 545257472 | bytes 19144704 | tf_op jit(solution)/shard_map/while/body/eval_jaxpr/gqhd,gjkhd->ghqjk/dot_general | solution.py:34
  190.7 8.5 %fusion.44 = f32[2,4,256]{2,1,0:T(4,128)S(1)} fusion(f32[2,4,256,8,256]{2,4,3,1,0:T(8,128)} %get-tuple-element.103, f32[2,4,256]{2,1,0:T(4,128)S(1)} %get-tuple-element.104), kind=kLoop, calls=%fused_computation.3.clone.1 | loop fusion | flops 12580864 | bytes 16793600 | tf_op jit(solution)/shard_map/while/body/eval_jaxpr/reduce_sum | solution.py:39
  199.3 7.5 %fusion.45 = bf16[4,2,256,4,64]{2,4,3,1,0:T(8,128)(2,1)S(1)} fusion(bf16[4,2,256,4,64]{2,4,3,1,0:T(8,128)(2,1)S(1)} %get-tuple-element.113, s32[]{:T(128)} %get-tuple-element.112, f32[2,4,256,8,256]{2,4,3,1,0:T(8,128)} %get-tuple-element.103, f32[2,4,256]{2,1,0:T(4,128)S(1)} %get-tuple-element.104, ...), kind=kOutput, calls=%fused_computation.15.clone.1 | convolution fusion | flops 549715968 | bytes 21250052 | tf_op jit(solution)/shard_map/while/body/eval_jaxpr/ghqjk,gjkhd->gqhd/dot_general | solution.py:41
  207.0 5.8 %gather_fusion = bf16[16,256,4,128]{3,1,2,0:T(8,128)(2,1)} fusion(bf16[24,256,4,128]{3,1,2,0:T(8,128)(2,1)} %get-tuple-element.121, s32[1024]{0:T(1024)S(1)} %pad_clamp_fusion.2), kind=kCustom, calls=%fused_computation.clone.1 | custom fusion | bytes 8388672 | tf_op jit(solution)/shard_map/while/body/eval_jaxpr/gather | solution.py:29
  212.8 5.0 %fusion.43 = (bf16[2,8,256,4,64]{4,2,3,1,0:T(8,128)(2,1)S(1)}, bf16[2,8,256,4,64]{4,2,3,1,0:T(8,128)(2,1)S(1)}) fusion(bf16[2,8,256,4,128]{4,2,3,1,0:T(8,128)(2,1)} %bitcast.60), kind=kLoop, calls=%fused_computation.23.clone.1 | loop fusion | bytes 8388608 | tf_op jit(solution)/shard_map/while/body/eval_jaxpr/slice | solution.py:32
  218.0 7.0 %multiply_reduce_fusion.2 = (f32[2,4,256]{2,1,0:T(4,128)S(1)}, f32[2,4,256,8,256]{2,4,3,1,0:T(8,128)}) fusion(bf16[2,8,256,4,64]{4,2,3,1,0:T(8,128)(2,1)S(1)} %get-tuple-element.102, bf16[1,2,256,4,64]{2,1,0,4,3:T(2,128)(2,1)S(1)} %constant_dynamic-slice_fusion.2), kind=kOutput, calls=%fused_computation.2.clone.1 | convolution fusion | flops 545257472 | bytes 19144704 | tf_op jit(solution)/shard_map/while/body/eval_jaxpr/gqhd,gjkhd->ghqjk/dot_general | solution.py:34
  225.0 8.5 %fusion.44 = f32[2,4,256]{2,1,0:T(4,128)S(1)} fusion(f32[2,4,256,8,256]{2,4,3,1,0:T(8,128)} %get-tuple-element.103, f32[2,4,256]{2,1,0:T(4,128)S(1)} %get-tuple-element.104), kind=kLoop, calls=%fused_computation.3.clone.1 | loop fusion | flops 12580864 | bytes 16793600 | tf_op jit(solution)/shard_map/while/body/eval_jaxpr/reduce_sum | solution.py:39
  233.5 7.5 %fusion.45 = bf16[4,2,256,4,64]{2,4,3,1,0:T(8,128)(2,1)S(1)} fusion(bf16[4,2,256,4,64]{2,4,3,1,0:T(8,128)(2,1)S(1)} %get-tuple-element.113, s32[]{:T(128)} %get-tuple-element.112, f32[2,4,256,8,256]{2,4,3,1,0:T(8,128)} %get-tuple-element.103, f32[2,4,256]{2,1,0:T(4,128)S(1)} %get-tuple-element.104, ...), kind=kOutput, calls=%fused_computation.15.clone.1 | convolution fusion | flops 549715968 | bytes 21250052 | tf_op jit(solution)/shard_map/while/body/eval_jaxpr/ghqjk,gjkhd->gqhd/dot_general | solution.py:41
  241.2 5.8 %gather_fusion = bf16[16,256,4,128]{3,1,2,0:T(8,128)(2,1)} fusion(bf16[24,256,4,128]{3,1,2,0:T(8,128)(2,1)} %get-tuple-element.121, s32[1024]{0:T(1024)S(1)} %pad_clamp_fusion.2), kind=kCustom, calls=%fused_computation.clone.1 | custom fusion | bytes 8388672 | tf_op jit(solution)/shard_map/while/body/eval_jaxpr/gather | solution.py:29
  252.3 7.0 %multiply_reduce_fusion.2 = (f32[2,4,256]{2,1,0:T(4,128)S(1)}, f32[2,4,256,8,256]{2,4,3,1,0:T(8,128)}) fusion(bf16[2,8,256,4,64]{4,2,3,1,0:T(8,128)(2,1)S(1)} %get-tuple-element.102, bf16[1,2,256,4,64]{2,1,0,4,3:T(2,128)(2,1)S(1)} %constant_dynamic-slice_fusion.2), kind=kOutput, calls=%fused_computation.2.clone.1 | convolution fusion | flops 545257472 | bytes 19144704 | tf_op jit(solution)/shard_map/while/body/eval_jaxpr/gqhd,gjkhd->ghqjk/dot_general | solution.py:34
  259.2 8.5 %fusion.44 = f32[2,4,256]{2,1,0:T(4,128)S(1)} fusion(f32[2,4,256,8,256]{2,4,3,1,0:T(8,128)} %get-tuple-element.103, f32[2,4,256]{2,1,0:T(4,128)S(1)} %get-tuple-element.104), kind=kLoop, calls=%fused_computation.3.clone.1 | loop fusion | flops 12580864 | bytes 16793600 | tf_op jit(solution)/shard_map/while/body/eval_jaxpr/reduce_sum | solution.py:39
  267.8 7.5 %fusion.45 = bf16[4,2,256,4,64]{2,4,3,1,0:T(8,128)(2,1)S(1)} fusion(bf16[4,2,256,4,64]{2,4,3,1,0:T(8,128)(2,1)S(1)} %get-tuple-element.113, s32[]{:T(128)} %get-tuple-element.112, f32[2,4,256,8,256]{2,4,3,1,0:T(8,128)} %get-tuple-element.103, f32[2,4,256]{2,1,0:T(4,128)S(1)} %get-tuple-element.104, ...), kind=kOutput, calls=%fused_computation.15.clone.1 | convolution fusion | flops 549715968 | bytes 21250052 | tf_op jit(solution)/shard_map/while/body/eval_jaxpr/ghqjk,gjkhd->gqhd/dot_general | solution.py:41
  275.9 17.9 %all_to_all.36 = bf16[8,256,256]{2,1,0:T(8,128)(2,1)S(1)} all-to-all(bf16[8,256,256]{2,1,0:T(8,128)(2,1)S(1)} %copy.35), channel_id=1, replica_groups=mesh['uly'=8,'blk'=4] {'uly'}, dimensions={0} | all-to-all | bytes 2097152 | tf_op jit(solution)/shard_map/all_to_all | solution.py:72
  (37 shorter events, 43.6 us)
Async XLA Ops:
  82.7 12.6 %copy-start.1 = (s32[8,8]{1,0:T(8,128)S(1)}, s32[8,8]{1,0:T(8,128)}, u32[]{:S(2)}) copy-start(s32[8,8]{1,0:T(8,128)} %param.5) | copy-start | bytes 772
  88.3 28.1 %collective-permute-start = (bf16[2048,4,128]{0,2,1:T(8,128)(2,1)}, bf16[2048,4,128]{0,2,1:T(8,128)(2,1)}, u32[]{:S(2)}, u32[]{:S(2)}) collective-permute-start(bf16[2048,4,128]{0,2,1:T(8,128)(2,1)} %slice.18), channel_id=1, source_target_pairs={{0,1},{1,2},{2,3},{4,5},{5,6},{6,7},{8,9},{9,10},{10,11},{12,13},{... | collective-permute-start | bytes 6291464 | tf_op jit(solution)/shard_map/ppermute | solution.py:19
  93.2 27.7 %collective-permute-start.1 = (bf16[2048,4,128]{0,2,1:T(8,128)(2,1)}, bf16[2048,4,128]{0,2,1:T(8,128)(2,1)}, u32[]{:S(2)}, u32[]{:S(2)}) collective-permute-start(bf16[2048,4,128]{0,2,1:T(8,128)(2,1)} %slice.18), channel_id=1, source_target_pairs={{1,0},{2,1},{3,2},{5,4},{6,5},{7,6},{9,8},{10,9},{11,10},{13,12},{... | collective-permute-start | bytes 6291464 | tf_op jit(solution)/shard_map/ppermute | solution.py:21
  129.3 9.1 %copy-start = (bf16[4,2,256,4,64]{2,4,3,1,0:T(8,128)(2,1)S(1)}, bf16[4,2,256,4,64]{2,4,3,1,0:T(8,128)(2,1)}, u32[]{:S(2)}) copy-start(bf16[4,2,256,4,64]{2,4,3,1,0:T(8,128)(2,1)} %custom-call.2) | copy-start | bytes 3145732
where the time goes:
time: 297 us; the launch traced here: 296 us
  blocking collectives  93.9 us (32%)
  local copies, waits for them, and re-layouts  75.9 us (26%)
  matrix products  58.1 us (20%)
  other arithmetic  37.9 us (13%)
  waiting for transfers between devices  22.6 us (8%)
  starting transfers between devices  6.9 us (2%)
    all_to_all x1, blocking collectives, on_device(): lax.all_to_all(qkv, 'uly', split_axis=1, concat_axis=0, tiled=True)  76 us
    reduce_sum x4, other arithmetic, attend_group(): row_sum = jnp.sum(exponent, axis=(3, 4))  34.2 us
    dot_general x4, matrix products, attend_group(): jnp.einsum('ghqjk,gjkhd->gqhd', weights, val_part, preferred_element_type...  30.2 us
    dot_general x4, matrix products, attend_group(): jnp.einsum('gqhd,gjkhd->ghqjk', queries, key_part, preferred_element_type...  27.9 us
    gather x4, local copies, waits for them, and re-layouts, attend_group(): picked = window[listed]  23.2 us
    slice x4, local copies, waits for them, and re-layouts, attend_group(): val_part = picked[..., head_width:]  20.1 us
    ppermute x1, waiting for transfers between devices, with_halo(): lax.ppermute(tail, axis, [(i, (i + 1) % count) for i in range(ends)])  18.2 us
    all_to_all x1, blocking collectives, on_device(): lax.all_to_all(result, 'uly', split_axis=0, concat_axis=1, tiled=True)  17.9 us
  transfers between devices with their start and end apart: 2, of which 2 were waited for; matrix products, arithmetic and copies ran while one was open for 1% of the time, Pallas kernels for 0%

commit v1 on v0

v1 whole, which is shorter than its diff:
```python
import functools

import jax
import jax.numpy as jnp
from jax import lax
from jax.experimental import pallas as pl
from jax.experimental.pallas import tpu as pltpu
from jax.sharding import PartitionSpec as P

HEAD_DIM = 64
LANES = 128
MESH = pl.DeviceIdType.MESH
SCORE_SCALE = HEAD_DIM ** -0.5
AHEAD = 2


def flip(me, mask, count):
    total, weight = 0, 1
    while weight < count:
        bit = lax.rem(lax.div(me, weight) + lax.div(mask, weight), 2)
        total = total + bit * weight
        weight *= 2
    return total


def attend_tile(list_ref, tile, first, query, wins, stage, head, scores):
    listed = list_ref.shape[1]
    lane = lax.broadcasted_iota(jnp.int32, query.shape, 1)
    moved = pltpu.roll(query.astype(jnp.float32), HEAD_DIM, 1) * SCORE_SCALE
    keep = lane >= HEAD_DIM if head == 0 else lane < HEAD_DIM
    moved = jnp.where(keep, moved, 0.0).astype(jnp.bfloat16)
    values_low = head == 0
    top = None
    for j in range(listed):
        index = jnp.clip(list_ref[tile, j] - first, 0, wins[stage].shape[0] - 1)
        keys = wins[stage][index, :, 0:LANES]
        part = lax.dot_general(
            moved, keys, (((1,), (1,)), ((), ())), preferred_element_type=jnp.float32
        )
        scores[j] = part
        for c in range(0, part.shape[1], LANES):
            piece = part[:, c:c + LANES]
            top = piece if top is None else jnp.maximum(top, piece)
    row_max = jnp.max(top, axis=1, keepdims=True)
    total = None
    for j in range(listed):
        index = jnp.clip(list_ref[tile, j] - first, 0, wins[stage].shape[0] - 1)
        weights = jnp.exp(scores[j] - row_max).astype(jnp.bfloat16)
        if head == 0:
            values = wins[stage][index, :, LANES:2 * LANES]
        else:
            values = wins[stage][index, :, 0:LANES]
        value_lane = lax.broadcasted_iota(jnp.int32, values.shape, 1)
        ones = value_lane >= HEAD_DIM if values_low else value_lane < HEAD_DIM
        values = jnp.where(ones, jnp.ones_like(values), values)
        part = lax.dot_general(
            weights, values, (((1,), (0,)), ((), ())), preferred_element_type=jnp.float32
        )
        total = part if total is None else total + part
    return total / pltpu.roll(total, HEAD_DIM, 1)


def kernel(ulys, blks, units, stages, unit_width, list_ref, qkv_ref, out_ref, *scratch):
    count = len(stages)
    wins = scratch[:count]
    outs = scratch[count:count + units]
    (scores, own_sem, in_send, in_recv, halo_send, halo_recv,
     out_own, out_send, out_recv) = scratch[count + units:]
    me = lax.axis_index("uly")
    blk = lax.axis_index("blk")
    first = (blk - 1) * ulys
    has_prev = blk > 0
    has_next = blk < blks - 1

    def peer(step):
        return flip(me, ulys - 1 - step, ulys)

    def columns(owner, stage):
        unit, _, begin, width = stages[stage]
        start = (owner * units + unit) * unit_width + begin
        return qkv_ref.at[:, pl.ds(pl.multiple_of(start, LANES), width)]

    def inbound(stage, other):
        return pltpu.make_async_remote_copy(
            src_ref=columns(other, stage),
            dst_ref=wins[stage].at[ulys + me],
            send_sem=in_send.at[stage, other],
            recv_sem=in_recv.at[stage, me],
            device_id={"uly": other},
            device_id_type=MESH,
        )

    def arrival(stage, other):
        return pltpu.make_async_remote_copy(
            src_ref=columns(other, stage),
            dst_ref=wins[stage].at[ulys + other],
            send_sem=in_send.at[stage, other],
            recv_sem=in_recv.at[stage, other],
            device_id={"uly": other},
            device_id_type=MESH,
        )

    def own(stage):
        return pltpu.make_async_copy(
            columns(me, stage), wins[stage].at[ulys + me], own_sem.at[stage]
        )

    def halo(stage, side, tile):
        return pltpu.make_async_remote_copy(
            src_ref=wins[stage].at[ulys + tile],
            dst_ref=wins[stage].at[2 * ulys * side + tile],
            send_sem=halo_send.at[stage, side, tile],
            recv_sem=halo_recv.at[stage, side, tile],
            device_id={"blk": blk + 1 - 2 * side},
            device_id_type=MESH,
        )

    def out_columns(owner, unit):
        start = (owner * units + unit) * LANES
        return out_ref.at[:, pl.ds(pl.multiple_of(start, LANES), LANES)]

    def outbound(unit, other):
        return pltpu.make_async_remote_copy(
            src_ref=outs[unit].at[other],
            dst_ref=out_columns(me, unit),
            send_sem=out_send.at[unit, other],
            recv_sem=out_recv.at[unit, me],
            device_id={"uly": other},
            device_id_type=MESH,
        )

    def returned(unit, other):
        return pltpu.make_async_remote_copy(
            src_ref=outs[unit].at[other],
            dst_ref=out_columns(other, unit),
            send_sem=out_send.at[unit, other],
            recv_sem=out_recv.at[unit, other],
            device_id={"uly": other},
            device_id_type=MESH,
        )

    def out_here(unit):
        return pltpu.make_async_copy(
            outs[unit].at[me], out_columns(me, unit), out_own.at[unit]
        )

    def forward(stage, tile):
        @pl.when(has_next)
        def _():
            halo(stage, 0, tile).start()

        @pl.when(has_prev)
        def _():
            halo(stage, 1, tile).start()

    def steps(limit, body):
        def run(step, carry):
            body(step)
            return carry
        lax.fori_loop(0, limit, run, 0)

    barrier = pltpu.get_barrier_semaphore()

    def greet(step):
        pl.semaphore_signal(
            barrier, inc=1, device_id={"uly": peer(step)}, device_id_type=MESH
        )

    steps(ulys - 1, greet)

    @pl.when(has_next)
    def _():
        pl.semaphore_signal(barrier, inc=1, device_id={"blk": blk + 1}, device_id_type=MESH)

    @pl.when(has_prev)
    def _():
        pl.semaphore_signal(barrier, inc=1, device_id={"blk": blk - 1}, device_id_type=MESH)

    beside = jnp.where(has_prev, 1, 0) + jnp.where(has_next, 1, 0)
    pl.semaphore_wait(barrier, ulys - 1 + beside)

    for stage in range(min(AHEAD, count)):
        steps(ulys - 1, lambda step, stage=stage: inbound(stage, peer(step)).start())
    for stage in range(count):
        own(stage).start()

    def compute(stage, tile):
        unit, head, _, _ = stages[stage]
        if head == 0:
            query = wins[stage][ulys + tile, :, 0:LANES]
        else:
            query = wins[stage - 1][ulys + tile, :, LANES:2 * LANES]
        result = attend_tile(list_ref, tile, first, query, wins, stage, head, scores)
        lane = lax.broadcasted_iota(jnp.int32, result.shape, 1)
        if head == 0:
            outs[unit][tile] = jnp.where(lane < HEAD_DIM, result, 0.0).astype(jnp.bfloat16)
        else:
            before = outs[unit][tile].astype(jnp.float32)
            outs[unit][tile] = jnp.where(lane < HEAD_DIM, before, result).astype(jnp.bfloat16)

    for turn in range(count + 1):
        done = turn - 1
        if turn < count:
            own(turn).wait()
            forward(turn, me)
        if done >= 0:
            def arrived(tile, done=done):
                @pl.when(has_prev)
                def _():
                    halo(done, 0, tile).wait_recv()

                @pl.when(has_next)
                def _():
                    halo(done, 1, tile).wait_recv()

            steps(ulys, arrived)

        def body(step, turn=turn, done=done):
            other = peer(step)
            if turn < count:
                @pl.when(step < ulys - 1)
                def _():
                    arrival(turn, other).wait_recv()
                    forward(turn, other)
                    if turn + AHEAD < count:
                        inbound(turn + AHEAD, other).start()
            if done >= 0:
                compute(done, other)
                unit = stages[done][0]
                if done == count - 1 or stages[done + 1][0] != unit:
                    @pl.when(step < ulys - 1)
                    def _():
                        outbound(unit, other).start()

                    @pl.when(step == ulys - 1)
                    def _():
                        out_here(unit).start()

        steps(ulys, body)

    def finish(step):
        other = peer(step)
        for stage in range(count):
            inbound(stage, other).wait_send()
        for unit in range(units):
            outbound(unit, other).wait_send()
            returned(unit, other).wait_recv()

    steps(ulys - 1, finish)

    def finish_halo(tile):
        for stage in range(count):
            @pl.when(has_next)
            def _():
                halo(stage, 0, tile).wait_send()

            @pl.when(has_prev)
            def _():
                halo(stage, 1, tile).wait_send()

    steps(ulys, finish_halo)
    for unit in range(units):
        out_here(unit).wait()


def on_device(qkv, tile_list):
    tokens, width = qkv.shape
    ulys, blks = lax.axis_size("uly"), lax.axis_size("blk")
    heads = width // (3 * HEAD_DIM)
    heads_here = heads // ulys
    paired = heads_here % 2 == 0
    if paired:
        units, unit_width = heads_here // 2, 6 * HEAD_DIM
        stages = []
        for unit in range(units):
            stages += [(unit, 0, 0, 2 * LANES), (unit, 1, 2 * LANES, LANES)]
    else:
        units, unit_width = heads_here, 4 * HEAD_DIM
        stages = [(unit, 0, 0, 2 * LANES) for unit in range(units)]
        qkv = jnp.pad(
            qkv.reshape(tokens, heads, 3 * HEAD_DIM), ((0, 0), (0, 0), (0, HEAD_DIM))
        ).reshape(tokens, heads * unit_width)
    listed = tile_list.shape[1]
    count = len(stages)
    out_width = ulys * units * LANES
    dma = pltpu.SemaphoreType.DMA
    pairs = ulys * listed * heads_here
    out = pl.pallas_call(
        functools.partial(kernel, ulys, blks, units, tuple(stages), unit_width),
        out_shape=jax.ShapeDtypeStruct((tokens, out_width), jnp.bfloat16),
        in_specs=[
            pl.BlockSpec(memory_space=pltpu.SMEM),
            pl.BlockSpec(memory_space=pl.ANY),
        ],
        out_specs=pl.BlockSpec(memory_space=pl.ANY),
        scratch_shapes=[
            pltpu.VMEM((3 * ulys, tokens, stage[3]), jnp.bfloat16) for stage in stages
        ] + [
            pltpu.VMEM((ulys, tokens, LANES), jnp.bfloat16) for _ in range(units)
        ] + [
            pltpu.VMEM((listed, tokens, tokens), jnp.float32),
            dma((count,)),
            dma((count, ulys)),
            dma((count, ulys)),
            dma((count, 2, ulys)),
            dma((count, 2, ulys)),
            dma((units,)),
            dma((units, ulys)),
            dma((units, ulys)),
        ],
        compiler_params=pltpu.CompilerParams(
            collective_id=0, has_side_effects=True, vmem_limit_bytes=48 * 1024 * 1024
        ),
        cost_estimate=pl.CostEstimate(
            flops=4 * pairs * tokens * tokens * HEAD_DIM,
            bytes_accessed=2 * qkv.size * 2,
            transcendentals=pairs * tokens * tokens,
        ),
    )(tile_list, qkv)
    if not paired:
        out = out.reshape(tokens, heads, LANES)[:, :, :HEAD_DIM]
        out = out.reshape(tokens, heads * HEAD_DIM)
    return out


def solution(mesh):
    in_specs = (P(("blk", "uly"), None), P("blk", None))
    out_specs = P(("blk", "uly"), None)
    return jax.shard_map(
        on_device, mesh=mesh, in_specs=in_specs, out_specs=out_specs, check_vma=False
    )
```

time: 297 us -> 107 us (0.36)
  Pallas kernels: 0 us -> 103 us
  blocking collectives: 93.9 us -> 0 us
  local copies, waits for them, and re-layouts: 75.9 us -> 3.55 us
  matrix products: 58.1 us -> 0 us
  other arithmetic: 37.9 us -> 0 us
  waiting for transfers between devices: 22.6 us -> 0 us
  starting transfers between devices: 6.9 us -> 0 us
    pallas_call x0 -> x1, Pallas kernels: none -> 103 us  [on_device(): pl.pallas_call(functools.partial(kernel, ulys, blks, units, tuple(stages)...]
    all_to_all x2 -> x0, blocking collectives: 93.9 us -> none  [the longest x1 76 us: on_device(): lax.all_to_all(qkv, 'uly', split_axis=1, concat_axis=0, tiled=True)]
    dot_general x8 -> x0, matrix products: 58.1 us -> none  [the longest x4 30.2 us: attend_group(): jnp.einsum('ghqjk,gjkhd->gqhd', weights, val_part, preferred_element_type...]
    reduce_sum x4 -> x0, other arithmetic: 34.2 us -> none  [attend_group(): row_sum = jnp.sum(exponent, axis=(3, 4))]
    gather x4 -> x0, local copies, waits for them, and re-layouts: 23.2 us -> none  [attend_group(): picked = window[listed]]
    slice x6 -> x0, local copies, waits for them, and re-layouts: 22.7 us -> none  [the longest x4 20.1 us: attend_group(): val_part = picked[..., head_width:]]
    ppermute x2 -> x0, waiting for transfers between devices: 22.6 us -> none  [the longest x1 18.2 us: with_halo(): lax.ppermute(tail, axis, [(i, (i + 1) % count) for i in range(ends)])]
    while x1 -> x0, local copies, waits for them, and re-layouts: 9.05 us -> none  [on_device(): result = lax.map(run_group, (query_groups, list_groups))]
  transfers between devices with their start and end apart: 2 -> 0, of which waited for: 2 -> 0; matrix products, arithmetic and copies ran while one was open for 1% -> 0% of each run, Pallas kernels for 0% -> 0%
where the time goes in v1:
time: 107 us
  Pallas kernels  103 us (96%)
  local copies, waits for them, and re-layouts  3.55 us (3%)
    pallas_call x1, Pallas kernels, on_device(): pl.pallas_call(functools.partial(kernel, ulys, blks, units, tuple(stages)...  103 us
    unnamed x5, local copies, waits for them, and re-layouts  3.55 us

profile of v1, /device:TPU:1, one launch (start us, length us, event | category | flops | bytes accessed | tf_op | source)
XLA Modules:
  0.0 106.6 jit_solution(1027547968934333508)
XLA Ops:
  0.0 0.0 copy-start
  0.0 1.9 %copy-done = bf16[256,6144]{1,0:T(8,128)(2,1)S(1)} copy-done((bf16[256,6144]{1,0:T(8,128)(2,1)S(1)}, bf16[256,6144]{1,0:T(8,128)(2,1)}, u32[]{:S(2)}) %copy-start) | copy-done | bytes 3145752
  1.9 0.0 copy-start.1
  1.9 0.7 copy-done.1
  2.6 103.0 %shard_map.28 = bf16[256,2048]{1,0:T(8,128)(2,1)S(1)} custom-call(s32[8,8]{1,0:T(8,128)S(1)} %copy-done.1, bf16[256,6144]{1,0:T(8,128)(2,1)S(1)} %copy-done), custom_call_target="tpu_custom_call" | custom-call | flops 4294967296 | bytes 6291456 | tf_op jit(solution)/shard_map/pallas_call | solution.py:288
  105.6 1.0 copy.4
Async XLA Ops:
  0.0 1.9 %copy-start = (bf16[256,6144]{1,0:T(8,128)(2,1)S(1)}, bf16[256,6144]{1,0:T(8,128)(2,1)}, u32[]{:S(2)}) copy-start(bf16[256,6144]{1,0:T(8,128)(2,1)} %qkv_ref.1) | copy-start | bytes 9437188
  1.9 0.7 copy-start.1

commit v2 on v1

--- a/solution.py
+++ b/solution.py
@@ -11,7 +11,7 @@
 LANES = 128
 MESH = pl.DeviceIdType.MESH
 SCORE_SCALE = HEAD_DIM ** -0.5
-AHEAD = 2
+AHEAD = 4
 
 
 def flip(me, mask, count):
@@ -60,12 +60,14 @@
     return total / pltpu.roll(total, HEAD_DIM, 1)
 
 
-def kernel(ulys, blks, units, stages, unit_width, list_ref, qkv_ref, out_ref, *scratch):
+def kernel(ulys, blks, units, stages, unit_width, list_hbm, qkv_ref, out_ref, *scratch):
     count = len(stages)
     wins = scratch[:count]
     outs = scratch[count:count + units]
-    (scores, own_sem, in_send, in_recv, halo_send, halo_recv,
+    (scores, list_ref, list_sem, own_sem, in_send, in_recv, halo_send, halo_recv,
      out_own, out_send, out_recv) = scratch[count + units:]
+    list_copy = pltpu.make_async_copy(list_hbm, list_ref, list_sem)
+    list_copy.start()
     me = lax.axis_index("uly")
     blk = lax.axis_index("blk")
     first = (blk - 1) * ulys
@@ -75,6 +77,13 @@
     def peer(step):
         return flip(me, ulys - 1 - step, ulys)
 
+    def mixed(step):
+        half, odd = lax.div(step, 2), lax.rem(step, 2)
+        return flip(me, odd * (half + 1) + (1 - odd) * (ulys - 1 - half), ulys)
+
+    def near(step):
+        return flip(me, step + 1, ulys)
+
     def columns(owner, stage):
         unit, _, begin, width = stages[stage]
         start = (owner * units + unit) * unit_width + begin
@@ -180,7 +189,7 @@
     pl.semaphore_wait(barrier, ulys - 1 + beside)
 
     for stage in range(min(AHEAD, count)):
-        steps(ulys - 1, lambda step, stage=stage: inbound(stage, peer(step)).start())
+        steps(ulys - 1, lambda step, stage=stage: inbound(stage, mixed(step)).start())
     for stage in range(count):
         own(stage).start()
 
@@ -198,6 +207,7 @@
             before = outs[unit][tile].astype(jnp.float32)
             outs[unit][tile] = jnp.where(lane < HEAD_DIM, before, result).astype(jnp.bfloat16)
 
+    list_copy.wait()
     for turn in range(count + 1):
         done = turn - 1
         if turn < count:
@@ -220,10 +230,11 @@
             if turn < count:
                 @pl.when(step < ulys - 1)
                 def _():
-                    arrival(turn, other).wait_recv()
-                    forward(turn, other)
+                    source = near(step)
+                    arrival(turn, source).wait_recv()
+                    forward(turn, source)
                     if turn + AHEAD < count:
-                        inbound(turn + AHEAD, other).start()
+                        inbound(turn + AHEAD, source).start()
             if done >= 0:
                 compute(done, other)
                 unit = stages[done][0]
@@ -289,8 +300,8 @@
         functools.partial(kernel, ulys, blks, units, tuple(stages), unit_width),
         out_shape=jax.ShapeDtypeStruct((tokens, out_width), jnp.bfloat16),
         in_specs=[
-            pl.BlockSpec(memory_space=pltpu.SMEM),
-            pl.BlockSpec(memory_space=pl.ANY),
+            pl.BlockSpec(memory_space=pltpu.HBM),
+            pl.BlockSpec(memory_space=pltpu.HBM),
         ],
         out_specs=pl.BlockSpec(memory_space=pl.ANY),
         scratch_shapes=[
@@ -299,6 +310,8 @@
             pltpu.VMEM((ulys, tokens, LANES), jnp.bfloat16) for _ in range(units)
         ] + [
             pltpu.VMEM((listed, tokens, tokens), jnp.float32),
+            pltpu.SMEM(tile_list.shape, jnp.int32),
+            dma(()),
             dma((count,)),
             dma((count, ulys)),
             dma((count, ulys)),
@@ -309,7 +322,7 @@
             dma((units, ulys)),
         ],
         compiler_params=pltpu.CompilerParams(
-            collective_id=0, has_side_effects=True, vmem_limit_bytes=48 * 1024 * 1024
+            collective_id=0, has_side_effects=True, vmem_limit_bytes=63 * 1024 * 1024
         ),
         cost_estimate=pl.CostEstimate(
             flops=4 * pairs * tokens * tokens * HEAD_DIM,

time: 107 us -> 105 us (0.981)
  local copies, waits for them, and re-layouts: 3.55 us -> 2.3 us
    unnamed x5 -> x1, local copies, waits for them, and re-layouts: 3.55 us -> 2.3 us
where the time goes in v2:
time: 105 us; the launch traced here: 104 us
  Pallas kernels  102 us (97%)
  local copies, waits for them, and re-layouts  2.3 us (2%)
    pallas_call x1, Pallas kernels, on_device(): pl.pallas_call(functools.partial(kernel, ulys, blks, units, tuple(stages)...  102 us
    unnamed x1, local copies, waits for them, and re-layouts  2.3 us

profile of v2, /device:TPU:1, one launch (start us, length us, event | category | flops | bytes accessed | tf_op | source)
XLA Modules:
  0.0 104.4 jit_solution(6245945980341077705)
XLA Ops:
  0.0 102.0 %shard_map.28 = bf16[256,2048]{1,0:T(8,128)(2,1)} custom-call(s32[8,8]{1,0:T(8,128)} %list_hbm.1, bf16[256,6144]{1,0:T(8,128)(2,1)} %qkv_ref.1), custom_call_target="tpu_custom_call" | custom-call | flops 4294967296 | bytes 6291456 | tf_op jit(solution)/shard_map/pallas_call | solution.py:299
  102.1 2.3 %copy.4 = bf16[256,2048]{1,0:T(8,128)(2,1)} copy(bf16[256,2048]{1,0:T(8,128)(2,1)} %shard_map.28) | data formatting | bytes 2097152

commit v3 on v2

--- a/solution.py
+++ b/solution.py
@@ -12,6 +12,7 @@
 MESH = pl.DeviceIdType.MESH
 SCORE_SCALE = HEAD_DIM ** -0.5
 AHEAD = 4
+ONES = 16
 
 
 def flip(me, mask, count):
@@ -23,48 +24,40 @@
     return total
 
 
-def attend_tile(list_ref, tile, first, query, wins, stage, head, scores):
+def attend_tile(list_ref, tile, first, query, window, turned, head, scores):
     listed = list_ref.shape[1]
-    lane = lax.broadcasted_iota(jnp.int32, query.shape, 1)
-    moved = pltpu.roll(query.astype(jnp.float32), HEAD_DIM, 1) * SCORE_SCALE
-    keep = lane >= HEAD_DIM if head == 0 else lane < HEAD_DIM
-    moved = jnp.where(keep, moved, 0.0).astype(jnp.bfloat16)
-    values_low = head == 0
+    last = window.shape[0] - 1
+    across = jnp.transpose(query)
+    blank = jnp.zeros((HEAD_DIM, across.shape[1]), jnp.bfloat16)
+    if head == 0:
+        part = across[:HEAD_DIM].astype(jnp.float32) * SCORE_SCALE
+        across = jnp.concatenate([blank, part.astype(jnp.bfloat16)], axis=0)
+    else:
+        part = across[HEAD_DIM:].astype(jnp.float32) * SCORE_SCALE
+        across = jnp.concatenate([part.astype(jnp.bfloat16), blank], axis=0)
     top = None
     for j in range(listed):
-        index = jnp.clip(list_ref[tile, j] - first, 0, wins[stage].shape[0] - 1)
-        keys = wins[stage][index, :, 0:LANES]
-        part = lax.dot_general(
-            moved, keys, (((1,), (1,)), ((), ())), preferred_element_type=jnp.float32
-        )
+        index = jnp.clip(list_ref[tile, j] - first, 0, last)
+        keys = window[index, :, 0:LANES]
+        part = jnp.dot(keys, across, preferred_element_type=jnp.float32)
         scores[j] = part
-        for c in range(0, part.shape[1], LANES):
-            piece = part[:, c:c + LANES]
-            top = piece if top is None else jnp.maximum(top, piece)
-    row_max = jnp.max(top, axis=1, keepdims=True)
+        piece = jnp.max(part.reshape(part.shape[0] // 8, 8, part.shape[1]), axis=0)
+        top = piece if top is None else jnp.maximum(top, piece)
+    col_max = jnp.max(top, axis=0, keepdims=True)
     total = None
     for j in range(listed):
-        index = jnp.clip(list_ref[tile, j] - first, 0, wins[stage].shape[0] - 1)
-        weights = jnp.exp(scores[j] - row_max).astype(jnp.bfloat16)
-        if head == 0:
-            values = wins[stage][index, :, LANES:2 * LANES]
-        else:
-            values = wins[stage][index, :, 0:LANES]
-        value_lane = lax.broadcasted_iota(jnp.int32, values.shape, 1)
-        ones = value_lane >= HEAD_DIM if values_low else value_lane < HEAD_DIM
-        values = jnp.where(ones, jnp.ones_like(values), values)
-        part = lax.dot_general(
-            weights, values, (((1,), (0,)), ((), ())), preferred_element_type=jnp.float32
-        )
+        index = jnp.clip(list_ref[tile, j] - first, 0, last)
+        weights = jnp.exp(scores[j] - col_max).astype(jnp.bfloat16)
+        part = jnp.dot(turned[index], weights, preferred_element_type=jnp.float32)
         total = part if total is None else total + part
-    return total / pltpu.roll(total, HEAD_DIM, 1)
+    return total[:HEAD_DIM] / total[HEAD_DIM:HEAD_DIM + 1]
 
 
 def kernel(ulys, blks, units, stages, unit_width, list_hbm, qkv_ref, out_ref, *scratch):
     count = len(stages)
     wins = scratch[:count]
     outs = scratch[count:count + units]
-    (scores, list_ref, list_sem, own_sem, in_send, in_recv, halo_send, halo_recv,
+    (scores, turned, half, list_ref, list_sem, own_sem, in_send, in_recv, halo_send, halo_recv,
      out_own, out_send, out_recv) = scratch[count + units:]
     list_copy = pltpu.make_async_copy(list_hbm, list_ref, list_sem)
     list_copy.start()
@@ -199,13 +192,27 @@
             query = wins[stage][ulys + tile, :, 0:LANES]
         else:
             query = wins[stage - 1][ulys + tile, :, LANES:2 * LANES]
-        result = attend_tile(list_ref, tile, first, query, wins, stage, head, scores)
-        lane = lax.broadcasted_iota(jnp.int32, result.shape, 1)
+        result = attend_tile(
+            list_ref, tile, first, query, wins[stage], turned, head, scores
+        ).astype(jnp.bfloat16)
         if head == 0:
-            outs[unit][tile] = jnp.where(lane < HEAD_DIM, result, 0.0).astype(jnp.bfloat16)
+            half[tile] = result
+        if closes(stage):
+            low = half[tile] if head == 1 else result
+            high = result if head == 1 else jnp.zeros_like(result)
+            outs[unit][tile] = jnp.transpose(jnp.concatenate([low, high], axis=0))
+
+    def closes(stage):
+        return stage == count - 1 or stages[stage + 1][0] != stages[stage][0]
+
+    def turn_values(stage, index):
+        head = stages[stage][1]
+        if head == 0:
+            values = jnp.transpose(wins[stage][index, :, LANES:2 * LANES])[:HEAD_DIM]
         else:
-            before = outs[unit][tile].astype(jnp.float32)
-            outs[unit][tile] = jnp.where(lane < HEAD_DIM, before, result).astype(jnp.bfloat16)
+            values = jnp.transpose(wins[stage][index, :, 0:LANES])[HEAD_DIM:]
+        ones = jnp.ones((ONES, values.shape[1]), jnp.bfloat16)
+        turned[index] = jnp.concatenate([values, ones], axis=0)
 
     list_copy.wait()
     for turn in range(count + 1):
@@ -224,6 +231,14 @@
                     halo(done, 1, tile).wait_recv()
 
             steps(ulys, arrived)
+            low = jnp.where(has_prev, 0, ulys)
+            high = jnp.where(has_next, 3 * ulys, 2 * ulys)
+
+            def turn_one(index, carry, done=done):
+                turn_values(done, index)
+                return carry
+
+            lax.fori_loop(low, high, turn_one, 0)
 
         def body(step, turn=turn, done=done):
             other = peer(step)
@@ -238,7 +253,7 @@
             if done >= 0:
                 compute(done, other)
                 unit = stages[done][0]
-                if done == count - 1 or stages[done + 1][0] != unit:
+                if closes(done):
                     @pl.when(step < ulys - 1)
                     def _():
                         outbound(unit, other).start()
@@ -310,6 +325,8 @@
             pltpu.VMEM((ulys, tokens, LANES), jnp.bfloat16) for _ in range(units)
         ] + [
             pltpu.VMEM((listed, tokens, tokens), jnp.float32),
+            pltpu.VMEM((3 * ulys, HEAD_DIM + ONES, tokens), jnp.bfloat16),
+            pltpu.VMEM((ulys, HEAD_DIM, tokens), jnp.bfloat16),
             pltpu.SMEM(tile_list.shape, jnp.int32),
             dma(()),
             dma((count,)),
@@ -322,7 +339,7 @@
             dma((units, ulys)),
         ],
         compiler_params=pltpu.CompilerParams(
-            collective_id=0, has_side_effects=True, vmem_limit_bytes=63 * 1024 * 1024
+            collective_id=0, has_side_effects=True, vmem_limit_bytes=62 * 1024 * 1024
         ),
         cost_estimate=pl.CostEstimate(
             flops=4 * pairs * tokens * tokens * HEAD_DIM,

time: 105 us -> 110 us (1.048)
  Pallas kernels: 102 us -> 106 us
    pallas_call x1, Pallas kernels: 102 us -> 106 us  [on_device(): pl.pallas_call(functools.partial(kernel, ulys, blks, units, tuple(stages)...]
where the time goes in v3:
time: 110 us; the launch traced here: 109 us
  Pallas kernels  106 us (96%)
  local copies, waits for them, and re-layouts  2.3 us (2%)
    pallas_call x1, Pallas kernels, on_device(): pl.pallas_call(functools.partial(kernel, ulys, blks, units, tuple(stages)...  106 us
    unnamed x1, local copies, waits for them, and re-layouts  2.3 us

profile of v3, /device:TPU:1, one launch (start us, length us, event | category | flops | bytes accessed | tf_op | source)
XLA Modules:
  0.0 108.7 jit_solution(16156032268168557915)
XLA Ops:
  0.0 106.4 %shard_map.28 = bf16[256,2048]{1,0:T(8,128)(2,1)} custom-call(s32[8,8]{1,0:T(8,128)} %list_hbm.1, bf16[256,6144]{1,0:T(8,128)(2,1)} %qkv_ref.1), custom_call_target="tpu_custom_call" | custom-call | flops 4294967296 | bytes 6291456 | tf_op jit(solution)/shard_map/pallas_call | solution.py:314
  106.4 2.3 %copy.4 = bf16[256,2048]{1,0:T(8,128)(2,1)} copy(bf16[256,2048]{1,0:T(8,128)(2,1)} %shard_map.28) | data formatting | bytes 2097152

commit v4 on v2

--- a/solution.py
+++ b/solution.py
@@ -225,20 +225,17 @@
 
             steps(ulys, arrived)
 
+        def take(step, turn=turn):
+            source = near(step)
+            arrival(turn, source).wait_recv()
+            forward(turn, source)
+
         def body(step, turn=turn, done=done):
             other = peer(step)
-            if turn < count:
-                @pl.when(step < ulys - 1)
-                def _():
-                    source = near(step)
-                    arrival(turn, source).wait_recv()
-                    forward(turn, source)
-                    if turn + AHEAD < count:
-                        inbound(turn + AHEAD, source).start()
             if done >= 0:
                 compute(done, other)
                 unit = stages[done][0]
-                if done == count - 1 or stages[done + 1][0] != unit:
+                if unit == units - 1 and done == count - 1:
                     @pl.when(step < ulys - 1)
                     def _():
                         outbound(unit, other).start()
@@ -247,7 +244,22 @@
                     def _():
                         out_here(unit).start()
 
+            if turn < count:
+                @pl.when(step < ulys // 2 - 1)
+                def _():
+                    take(step)
+
         steps(ulys, body)
+        if turn < count:
+            steps(ulys // 2, lambda step, take=take: take(step + ulys // 2 - 1))
+        if turn == count - 1:
+            def early(step):
+                for unit in range(units - 1):
+                    outbound(unit, peer(step)).start()
+
+            steps(ulys - 1, early)
+            for unit in range(units - 1):
+                out_here(unit).start()
 
     def finish(step):
         other = peer(step)
@@ -322,7 +334,7 @@
             dma((units, ulys)),
         ],
         compiler_params=pltpu.CompilerParams(
-            collective_id=0, has_side_effects=True, vmem_limit_bytes=63 * 1024 * 1024
+            collective_id=0, has_side_effects=True, vmem_limit_bytes=50 * 1024 * 1024
         ),
         cost_estimate=pl.CostEstimate(
             flops=4 * pairs * tokens * tokens * HEAD_DIM,

time: 105 us -> 106 us (level)
    unnamed x1 -> x3, local copies, waits for them, and re-layouts: 2.3 us -> 1.66 us
where the time goes in v4:
time: 106 us; the launch traced here: 105 us
  Pallas kernels  103 us (97%)
  local copies, waits for them, and re-layouts  1.66 us (2%)
    pallas_call x1, Pallas kernels, on_device(): pl.pallas_call(functools.partial(kernel, ulys, blks, units, tuple(stages)...  103 us

profile of v4, /device:TPU:1, one launch (start us, length us, event | category | flops | bytes accessed | tf_op | source)
XLA Modules:
  0.0 104.8 jit_solution(10818197654071001411)
XLA Ops:
  0.0 0.0 copy-start
  0.0 0.7 copy-done
  0.7 103.1 %shard_map.28 = bf16[256,2048]{1,0:T(8,128)(2,1)S(1)} custom-call(s32[8,8]{1,0:T(8,128)S(1)} %copy-done, bf16[256,6144]{1,0:T(8,128)(2,1)} %qkv_ref.1), custom_call_target="tpu_custom_call" | custom-call | flops 4294967296 | bytes 6291456 | tf_op jit(solution)/shard_map/pallas_call | solution.py:311
  103.8 1.0 copy.4
Async XLA Ops:
  0.0 0.7 copy-start

commit v5 on v4

--- a/solution.py
+++ b/solution.py
@@ -23,48 +23,55 @@
     return total
 
 
-def attend_tile(list_ref, tile, first, query, wins, stage, head, scores):
+def attend_step(list_ref, first, window, value_at, head, now, later):
     listed = list_ref.shape[1]
-    lane = lax.broadcasted_iota(jnp.int32, query.shape, 1)
-    moved = pltpu.roll(query.astype(jnp.float32), HEAD_DIM, 1) * SCORE_SCALE
-    keep = lane >= HEAD_DIM if head == 0 else lane < HEAD_DIM
-    moved = jnp.where(keep, moved, 0.0).astype(jnp.bfloat16)
-    values_low = head == 0
+    last = window.shape[0] - 1
+    if later is not None:
+        next_tile, query, next_scores, next_maxima = later
+        lane = lax.broadcasted_iota(jnp.int32, query.shape, 1)
+        moved = pltpu.roll(query.astype(jnp.float32), HEAD_DIM, 1) * SCORE_SCALE
+        keep = lane >= HEAD_DIM if head == 0 else lane < HEAD_DIM
+        moved = jnp.where(keep, moved, 0.0).astype(jnp.bfloat16)
     top = None
-    for j in range(listed):
-        index = jnp.clip(list_ref[tile, j] - first, 0, wins[stage].shape[0] - 1)
-        keys = wins[stage][index, :, 0:LANES]
-        part = lax.dot_general(
-            moved, keys, (((1,), (1,)), ((), ())), preferred_element_type=jnp.float32
-        )
-        scores[j] = part
-        for c in range(0, part.shape[1], LANES):
-            piece = part[:, c:c + LANES]
-            top = piece if top is None else jnp.maximum(top, piece)
-    row_max = jnp.max(top, axis=1, keepdims=True)
     total = None
     for j in range(listed):
-        index = jnp.clip(list_ref[tile, j] - first, 0, wins[stage].shape[0] - 1)
-        weights = jnp.exp(scores[j] - row_max).astype(jnp.bfloat16)
-        if head == 0:
-            values = wins[stage][index, :, LANES:2 * LANES]
-        else:
-            values = wins[stage][index, :, 0:LANES]
-        value_lane = lax.broadcasted_iota(jnp.int32, values.shape, 1)
-        ones = value_lane >= HEAD_DIM if values_low else value_lane < HEAD_DIM
-        values = jnp.where(ones, jnp.ones_like(values), values)
-        part = lax.dot_general(
-            weights, values, (((1,), (0,)), ((), ())), preferred_element_type=jnp.float32
-        )
-        total = part if total is None else total + part
-    return total / pltpu.roll(total, HEAD_DIM, 1)
+        if later is not None:
+            index = jnp.clip(list_ref[next_tile, j] - first, 0, last)
+            keys = window[index, :, 0:LANES]
+            part = lax.dot_general(
+                moved, keys, (((1,), (1,)), ((), ())), preferred_element_type=jnp.float32
+            )
+            next_scores[j] = part
+            for c in range(0, part.shape[1], LANES):
+                piece = part[:, c:c + LANES]
+                top = piece if top is None else jnp.maximum(top, piece)
+        if now is not None:
+            tile, scores, maxima = now
+            index = jnp.clip(list_ref[tile, j] - first, 0, last)
+            weights = jnp.concatenate(
+                [
+                    jnp.exp(scores[j, :, c:c + LANES] - maxima[...]).astype(jnp.bfloat16)
+                    for c in range(0, scores.shape[2], LANES)
+                ],
+                axis=1,
+            )
+            values = window[index, :, value_at:value_at + LANES]
+            lane = lax.broadcasted_iota(jnp.int32, values.shape, 1)
+            ones = lane >= HEAD_DIM if head == 0 else lane < HEAD_DIM
+            values = jnp.where(ones, jnp.ones_like(values), values)
+            part = jnp.dot(weights, values, preferred_element_type=jnp.float32)
+            total = part if total is None else total + part
+    if later is not None:
+        next_maxima[...] = jnp.broadcast_to(jnp.max(top, axis=1, keepdims=True), top.shape)
+    if now is not None:
+        return total / pltpu.roll(total, HEAD_DIM, 1)
 
 
 def kernel(ulys, blks, units, stages, unit_width, list_hbm, qkv_ref, out_ref, *scratch):
     count = len(stages)
     wins = scratch[:count]
     outs = scratch[count:count + units]
-    (scores, list_ref, list_sem, own_sem, in_send, in_recv, halo_send, halo_recv,
+    (scores_a, scores_b, maxima_a, maxima_b, list_ref, list_sem, own_sem, in_send, in_recv, halo_send, halo_recv,
      out_own, out_send, out_recv) = scratch[count + units:]
     list_copy = pltpu.make_async_copy(list_hbm, list_ref, list_sem)
     list_copy.start()
@@ -193,19 +200,45 @@
     for stage in range(count):
         own(stage).start()
 
-    def compute(stage, tile):
+    def closes(stage):
+        return stage == count - 1 or stages[stage + 1][0] != stages[stage][0]
+
+    def attend(stage, now, later):
         unit, head, _, _ = stages[stage]
-        if head == 0:
-            query = wins[stage][ulys + tile, :, 0:LANES]
-        else:
-            query = wins[stage - 1][ulys + tile, :, LANES:2 * LANES]
-        result = attend_tile(list_ref, tile, first, query, wins, stage, head, scores)
+        tile = None
+        if now is not None:
+            tile = peer(now[0])
+            now = (tile,) + now[1:]
+        if later is not None:
+            following = peer(later[0])
+            if head == 0:
+                query = wins[stage][ulys + following, :, 0:LANES]
+            else:
+                query = wins[stage - 1][ulys + following, :, LANES:2 * LANES]
+            later = (following, query) + later[1:]
+        value_at = LANES if head == 0 else 0
+        result = attend_step(
+            list_ref, first, wins[stage], value_at, head, now, later
+        )
+        if tile is None:
+            return
         lane = lax.broadcasted_iota(jnp.int32, result.shape, 1)
         if head == 0:
             outs[unit][tile] = jnp.where(lane < HEAD_DIM, result, 0.0).astype(jnp.bfloat16)
         else:
             before = outs[unit][tile].astype(jnp.float32)
             outs[unit][tile] = jnp.where(lane < HEAD_DIM, before, result).astype(jnp.bfloat16)
+
+    def give(stage, step):
+        unit = stages[stage][0]
+        if closes(stage):
+            @pl.when(step < ulys - 1)
+            def _():
+                outbound(unit, peer(step)).start()
+
+            @pl.when(step == ulys - 1)
+            def _():
+                out_here(unit).start()
 
     list_copy.wait()
     for turn in range(count + 1):
@@ -230,36 +263,25 @@
             arrival(turn, source).wait_recv()
             forward(turn, source)
 
-        def body(step, turn=turn, done=done):
-            other = peer(step)
+        if done >= 0:
+            attend(done, None, (0, scores_a, maxima_a))
+
+        def body(pair, turn=turn, done=done):
             if done >= 0:
-                compute(done, other)
-                unit = stages[done][0]
-                if unit == units - 1 and done == count - 1:
-                    @pl.when(step < ulys - 1)
-                    def _():
-                        outbound(unit, other).start()
-
-                    @pl.when(step == ulys - 1)
-                    def _():
-                        out_here(unit).start()
-
+                even = 2 * pair
+                after = jnp.minimum(even + 2, ulys - 1)
+                attend(done, (even, scores_a, maxima_a), (even + 1, scores_b, maxima_b))
+                give(done, even)
+                attend(done, (even + 1, scores_b, maxima_b), (after, scores_a, maxima_a))
+                give(done, even + 1)
             if turn < count:
-                @pl.when(step < ulys // 2 - 1)
+                @pl.when(pair < ulys // 2 - 1)
                 def _():
-                    take(step)
-
-        steps(ulys, body)
+                    take(pair)
+
+        steps(ulys // 2, body)
         if turn < count:
             steps(ulys // 2, lambda step, take=take: take(step + ulys // 2 - 1))
-        if turn == count - 1:
-            def early(step):
-                for unit in range(units - 1):
-                    outbound(unit, peer(step)).start()
-
-            steps(ulys - 1, early)
-            for unit in range(units - 1):
-                out_here(unit).start()
 
     def finish(step):
         other = peer(step)
@@ -322,6 +344,9 @@
             pltpu.VMEM((ulys, tokens, LANES), jnp.bfloat16) for _ in range(units)
         ] + [
             pltpu.VMEM((listed, tokens, tokens), jnp.float32),
+            pltpu.VMEM((listed, tokens, tokens), jnp.float32),
+            pltpu.VMEM((tokens, LANES), jnp.float32),
+            pltpu.VMEM((tokens, LANES), jnp.float32),
             pltpu.SMEM(tile_list.shape, jnp.int32),
             dma(()),
             dma((count,)),

time: 106 us -> 110 us (1.038); the launches traced: 105 us -> 110 us
  Pallas kernels: 103 us -> 108 us
    pallas_call x1, Pallas kernels: 103 us -> 108 us  [on_device(): pl.pallas_call(functools.partial(kernel, ulys, blks, units, tuple(stages)...]
where the time goes in v5:
time: 110 us
  Pallas kernels  108 us (98%)
  local copies, waits for them, and re-layouts  1.66 us (2%)
    pallas_call x1, Pallas kernels, on_device(): pl.pallas_call(functools.partial(kernel, ulys, blks, units, tuple(stages)...  108 us

profile of v5, /device:TPU:1, one launch (start us, length us, event | category | flops | bytes accessed | tf_op | source)
XLA Modules:
  0.0 110.2 jit_solution(3626180194174598753)
XLA Ops:
  0.0 0.0 copy-start
  0.0 0.7 copy-done
  0.7 108.5 %shard_map.28 = bf16[256,2048]{1,0:T(8,128)(2,1)S(1)} custom-call(s32[8,8]{1,0:T(8,128)S(1)} %copy-done, bf16[256,6144]{1,0:T(8,128)(2,1)} %qkv_ref.1), custom_call_target="tpu_custom_call" | custom-call | flops 4294967296 | bytes 6291456 | tf_op jit(solution)/shard_map/pallas_call | solution.py:333
  109.2 1.0 copy.4
Async XLA Ops:
  0.0 0.7 copy-start

commit v6 on v2

--- a/solution.py
+++ b/solution.py
@@ -30,10 +30,11 @@
     keep = lane >= HEAD_DIM if head == 0 else lane < HEAD_DIM
     moved = jnp.where(keep, moved, 0.0).astype(jnp.bfloat16)
     values_low = head == 0
+    begin = wins[stage].shape[2] - LANES
     top = None
     for j in range(listed):
         index = jnp.clip(list_ref[tile, j] - first, 0, wins[stage].shape[0] - 1)
-        keys = wins[stage][index, :, 0:LANES]
+        keys = wins[stage][index, :, begin:begin + LANES]
         part = lax.dot_general(
             moved, keys, (((1,), (1,)), ((), ())), preferred_element_type=jnp.float32
         )
@@ -46,10 +47,7 @@
     for j in range(listed):
         index = jnp.clip(list_ref[tile, j] - first, 0, wins[stage].shape[0] - 1)
         weights = jnp.exp(scores[j] - row_max).astype(jnp.bfloat16)
-        if head == 0:
-            values = wins[stage][index, :, LANES:2 * LANES]
-        else:
-            values = wins[stage][index, :, 0:LANES]
+        values = wins[stage][index, :, begin:begin + LANES]
         value_lane = lax.broadcasted_iota(jnp.int32, values.shape, 1)
         ones = value_lane >= HEAD_DIM if values_low else value_lane < HEAD_DIM
         values = jnp.where(ones, jnp.ones_like(values), values)
@@ -60,14 +58,16 @@
     return total / pltpu.roll(total, HEAD_DIM, 1)
 
 
-def kernel(ulys, blks, units, stages, unit_width, list_hbm, qkv_ref, out_ref, *scratch):
+def kernel(ulys, blks, units, stages, unit_width, list_hbm, qkv_hbm, out_ref, *scratch):
     count = len(stages)
     wins = scratch[:count]
     outs = scratch[count:count + units]
-    (scores, list_ref, list_sem, own_sem, in_send, in_recv, halo_send, halo_recv,
+    (scores, qkv_ref, qkv_sem, list_ref, list_sem, own_sem, in_send, in_recv, halo_send, halo_recv,
      out_own, out_send, out_recv) = scratch[count + units:]
     list_copy = pltpu.make_async_copy(list_hbm, list_ref, list_sem)
     list_copy.start()
+    qkv_copy = pltpu.make_async_copy(qkv_hbm, qkv_ref, qkv_sem)
+    qkv_copy.start()
     me = lax.axis_index("uly")
     blk = lax.axis_index("blk")
     first = (blk - 1) * ulys
@@ -115,9 +115,11 @@
         )
 
     def halo(stage, side, tile):
-        return pltpu.make_async_remote_copy(
-            src_ref=wins[stage].at[ulys + tile],
-            dst_ref=wins[stage].at[2 * ulys * side + tile],
+        width = stages[stage][3]
+        pair = pl.ds(width - LANES, LANES)
+        return pltpu.make_async_remote_copy(
+            src_ref=wins[stage].at[ulys + tile, :, pair],
+            dst_ref=wins[stage].at[2 * ulys * side + tile, :, pair],
             send_sem=halo_send.at[stage, side, tile],
             recv_sem=halo_recv.at[stage, side, tile],
             device_id={"blk": blk + 1 - 2 * side},
@@ -188,6 +190,17 @@
     beside = jnp.where(has_prev, 1, 0) + jnp.where(has_next, 1, 0)
     pl.semaphore_wait(barrier, ulys - 1 + beside)
 
+    qkv_copy.wait()
+
+    def regroup(unit):
+        start = pl.multiple_of(unit * unit_width, LANES)
+        low = qkv_ref[:, pl.ds(start, LANES)]
+        high = qkv_ref[:, pl.ds(start + LANES, LANES)]
+        left = lax.broadcasted_iota(jnp.int32, low.shape, 1) < HEAD_DIM
+        qkv_ref[:, pl.ds(start, LANES)] = jnp.where(left, low, high)
+        qkv_ref[:, pl.ds(start + LANES, LANES)] = jnp.where(left, high, low)
+
+    steps(ulys * units, regroup)
     for stage in range(min(AHEAD, count)):
         steps(ulys - 1, lambda step, stage=stage: inbound(stage, mixed(step)).start())
     for stage in range(count):
@@ -198,7 +211,7 @@
         if head == 0:
             query = wins[stage][ulys + tile, :, 0:LANES]
         else:
-            query = wins[stage - 1][ulys + tile, :, LANES:2 * LANES]
+            query = wins[stage - 1][ulys + tile, :, 0:LANES]
         result = attend_tile(list_ref, tile, first, query, wins, stage, head, scores)
         lane = lax.broadcasted_iota(jnp.int32, result.shape, 1)
         if head == 0:
@@ -310,6 +323,8 @@
             pltpu.VMEM((ulys, tokens, LANES), jnp.bfloat16) for _ in range(units)
         ] + [
             pltpu.VMEM((listed, tokens, tokens), jnp.float32),
+            pltpu.VMEM(qkv.shape, jnp.bfloat16),
+            dma(()),
             pltpu.SMEM(tile_list.shape, jnp.int32),
             dma(()),
             dma((count,)),
@@ -322,7 +337,7 @@
             dma((units, ulys)),
         ],
         compiler_params=pltpu.CompilerParams(
-            collective_id=0, has_side_effects=True, vmem_limit_bytes=63 * 1024 * 1024
+            collective_id=0, has_side_effects=True, vmem_limit_bytes=50 * 1024 * 1024
         ),
         cost_estimate=pl.CostEstimate(
             flops=4 * pairs * tokens * tokens * HEAD_DIM,

time: 105 us -> 104 us (level)
    unnamed x1 -> x3, local copies, waits for them, and re-layouts: 2.3 us -> 1.66 us
where the time goes in v6:
time: 104 us
  Pallas kernels  102 us (98%)
  local copies, waits for them, and re-layouts  1.66 us (2%)
    pallas_call x1, Pallas kernels, on_device(): pl.pallas_call(functools.partial(kernel, ulys, blks, units, tuple(stages)...  102 us

profile of v6, /device:TPU:1, one launch (start us, length us, event | category | flops | bytes accessed | tf_op | source)
XLA Modules:
  0.0 103.7 jit_solution(7765323063647741865)
XLA Ops:
  0.0 0.0 copy-start
  0.0 0.7 copy-done
  0.7 102.0 %shard_map.28 = bf16[256,2048]{1,0:T(8,128)(2,1)S(1)} custom-call(s32[8,8]{1,0:T(8,128)S(1)} %copy-done, bf16[256,6144]{1,0:T(8,128)(2,1)} %qkv_hbm.1), custom_call_target="tpu_custom_call" | custom-call | flops 4294967296 | bytes 6291456 | tf_op jit(solution)/shard_map/pallas_call | solution.py:312
  102.7 1.0 copy.4
Async XLA Ops:
  0.0 0.7 copy-start

commit v7 on v6

--- a/solution.py
+++ b/solution.py
@@ -11,7 +11,6 @@
 LANES = 128
 MESH = pl.DeviceIdType.MESH
 SCORE_SCALE = HEAD_DIM ** -0.5
-AHEAD = 4
 
 
 def flip(me, mask, count):
@@ -62,8 +61,9 @@
     count = len(stages)
     wins = scratch[:count]
     outs = scratch[count:count + units]
-    (scores, qkv_ref, qkv_sem, list_ref, list_sem, own_sem, in_send, in_recv, halo_send, halo_recv,
-     out_own, out_send, out_recv) = scratch[count + units:]
+    relays = scratch[count + units:2 * count + units]
+    (relay_send, relay_recv, scores, qkv_ref, qkv_sem, list_ref, list_sem, own_sem, in_send, in_recv, halo_send, halo_recv,
+     out_own, out_send, out_recv) = scratch[2 * count + units:]
     list_copy = pltpu.make_async_copy(list_hbm, list_ref, list_sem)
     list_copy.start()
     qkv_copy = pltpu.make_async_copy(qkv_hbm, qkv_ref, qkv_sem)
@@ -77,10 +77,6 @@
     def peer(step):
         return flip(me, ulys - 1 - step, ulys)
 
-    def mixed(step):
-        half, odd = lax.div(step, 2), lax.rem(step, 2)
-        return flip(me, odd * (half + 1) + (1 - odd) * (ulys - 1 - half), ulys)
-
     def near(step):
         return flip(me, step + 1, ulys)
 
@@ -98,6 +94,48 @@
             device_id={"uly": other},
             device_id_type=MESH,
         )
+
+    half = ulys // 2
+    low = lax.rem(me, 2)
+    mine = lax.div(me, 2)
+    partner = me + 1 - 2 * low
+
+    def place(step):
+        return flip(mine, half - 1 - step, half)
+
+    def first_leg(stage, to):
+        owner = 2 * to + 1 - low
+        return pltpu.make_async_remote_copy(
+            src_ref=columns(owner, stage),
+            dst_ref=relays[stage].at[to],
+            send_sem=in_send.at[stage, owner],
+            recv_sem=relay_recv.at[stage, to],
+            device_id={"uly": partner},
+            device_id_type=MESH,
+        )
+
+    def second_leg(stage, to):
+        return pltpu.make_async_remote_copy(
+            src_ref=relays[stage].at[to],
+            dst_ref=wins[stage].at[ulys + partner],
+            send_sem=relay_send.at[stage, to],
+            recv_sem=in_recv.at[stage, partner],
+            device_id={"uly": 2 * to + low},
+            device_id_type=MESH,
+        )
+
+    def send_out(stage):
+        def one(step):
+            first_leg(stage, place(step)).start()
+            inbound(stage, 2 * place(step) + low).start()
+        steps(half - 1, one)
+        inbound(stage, partner).start()
+
+    def pass_on(stage):
+        def one(step):
+            first_leg(stage, place(step)).wait_recv()
+            second_leg(stage, place(step)).start()
+        steps(half - 1, one)
 
     def arrival(stage, other):
         return pltpu.make_async_remote_copy(
@@ -201,8 +239,8 @@
         qkv_ref[:, pl.ds(start + LANES, LANES)] = jnp.where(left, high, low)
 
     steps(ulys * units, regroup)
-    for stage in range(min(AHEAD, count)):
-        steps(ulys - 1, lambda step, stage=stage: inbound(stage, mixed(step)).start())
+    for stage in range(count):
+        send_out(stage)
     for stage in range(count):
         own(stage).start()
 
@@ -221,9 +259,13 @@
             outs[unit][tile] = jnp.where(lane < HEAD_DIM, before, result).astype(jnp.bfloat16)
 
     list_copy.wait()
+    for stage in range(min(2, count)):
+        pass_on(stage)
     for turn in range(count + 1):
         done = turn - 1
         if turn < count:
+            if turn + 2 < count:
+                pass_on(turn + 2)
             own(turn).wait()
             forward(turn, me)
         if done >= 0:
@@ -246,8 +288,6 @@
                     source = near(step)
                     arrival(turn, source).wait_recv()
                     forward(turn, source)
-                    if turn + AHEAD < count:
-                        inbound(turn + AHEAD, source).start()
             if done >= 0:
                 compute(done, other)
                 unit = stages[done][0]
@@ -283,6 +323,12 @@
                 halo(stage, 1, tile).wait_send()
 
     steps(ulys, finish_halo)
+
+    def finish_legs(step):
+        for stage in range(count):
+            second_leg(stage, place(step)).wait_send()
+
+    steps(half - 1, finish_legs)
     for unit in range(units):
         out_here(unit).wait()
 
@@ -322,6 +368,10 @@
         ] + [
             pltpu.VMEM((ulys, tokens, LANES), jnp.bfloat16) for _ in range(units)
         ] + [
+            pltpu.VMEM((ulys // 2, tokens, stage[3]), jnp.bfloat16) for stage in stages
+        ] + [
+            dma((count, ulys // 2)),
+            dma((count, ulys // 2)),
             pltpu.VMEM((listed, tokens, tokens), jnp.float32),
             pltpu.VMEM(qkv.shape, jnp.bfloat16),
             dma(()),

time: 104 us -> 108 us (1.038)
  Pallas kernels: 102 us -> 106 us
    pallas_call x1, Pallas kernels: 102 us -> 106 us  [on_device(): pl.pallas_call(functools.partial(kernel, ulys, blks, units, tuple(stages)...]
where the time goes in v7:
time: 108 us
  Pallas kernels  106 us (98%)
  local copies, waits for them, and re-layouts  1.66 us (2%)
    pallas_call x1, Pallas kernels, on_device(): pl.pallas_call(functools.partial(kernel, ulys, blks, units, tuple(stages)...  106 us

profile of v7, /device:TPU:1, one launch (start us, length us, event | category | flops | bytes accessed | tf_op | source)
XLA Modules:
  0.0 107.7 jit_solution(17037626889490605973)
XLA Ops:
  0.0 0.0 copy-start
  0.0 0.7 copy-done
  0.7 106.0 %shard_map.28 = bf16[256,2048]{1,0:T(8,128)(2,1)S(1)} custom-call(s32[8,8]{1,0:T(8,128)S(1)} %copy-done, bf16[256,6144]{1,0:T(8,128)(2,1)} %qkv_hbm.1), custom_call_target="tpu_custom_call" | custom-call | flops 4294967296 | bytes 6291456 | tf_op jit(solution)/shard_map/pallas_call | solution.py:358
  106.7 1.0 copy.4
Async XLA Ops:
  0.0 0.7 copy-start

commit v8 on v6

--- a/solution.py
+++ b/solution.py
@@ -238,16 +238,13 @@
 
             steps(ulys, arrived)
 
+        def take(step, turn=turn):
+            source = near(step)
+            arrival(turn, source).wait_recv()
+            forward(turn, source)
+
         def body(step, turn=turn, done=done):
             other = peer(step)
-            if turn < count:
-                @pl.when(step < ulys - 1)
-                def _():
-                    source = near(step)
-                    arrival(turn, source).wait_recv()
-                    forward(turn, source)
-                    if turn + AHEAD < count:
-                        inbound(turn + AHEAD, source).start()
             if done >= 0:
                 compute(done, other)
                 unit = stages[done][0]
@@ -260,7 +257,14 @@
                     def _():
                         out_here(unit).start()
 
+            if turn < count:
+                @pl.when(step < ulys // 2 - 1)
+                def _():
+                    take(step)
+
         steps(ulys, body)
+        if turn < count:
+            steps(ulys // 2, lambda step, take=take: take(step + ulys // 2 - 1))
 
     def finish(step):
         other = peer(step)

time: 104 us -> 108 us (1.038); the launches traced: 104 us -> 106 us
  Pallas kernels: 102 us -> 105 us
    pallas_call x1, Pallas kernels: 102 us -> 105 us  [on_device(): pl.pallas_call(functools.partial(kernel, ulys, blks, units, tuple(stages)...]
where the time goes in v8:
time: 108 us; the launch traced here: 106 us
  Pallas kernels  105 us (97%)
  local copies, waits for them, and re-layouts  1.66 us (2%)
    pallas_call x1, Pallas kernels, on_device(): pl.pallas_call(functools.partial(kernel, ulys, blks, units, tuple(stages)...  105 us

profile of v8, /device:TPU:1, one launch (start us, length us, event | category | flops | bytes accessed | tf_op | source)
XLA Modules:
  0.0 106.2 jit_solution(2108249499281114346)
XLA Ops:
  0.0 0.0 copy-start
  0.0 0.7 copy-done
  0.7 104.6 %shard_map.28 = bf16[256,2048]{1,0:T(8,128)(2,1)S(1)} custom-call(s32[8,8]{1,0:T(8,128)S(1)} %copy-done, bf16[256,6144]{1,0:T(8,128)(2,1)} %qkv_hbm.1), custom_call_target="tpu_custom_call" | custom-call | flops 4294967296 | bytes 6291456 | tf_op jit(solution)/shard_map/pallas_call | solution.py:316
  105.3 1.0 copy.4
Async XLA Ops:
  0.0 0.7 copy-start
